TPU v7x, 32 devices: a whole 2x2x4 slice. The times are simulated.
32 devices in a mesh: dc: 8 (over y, x, core), tp: 4 (over z).
Axes of the slice: x: 2, y: 2, z: 4, core: 2. Of those that a mesh axis runs over, the one named last changes fastest.
Arguments:
- queries: bfloat16 [1536, 1024], P('dc', 'tp'), may hold values from -15 to 15
- keys: bfloat16 [1536, 256], P('dc'), may hold values from -4.5 to 4.5
- values: bfloat16 [1536, 256], P('dc'), may hold values from -5 to 5
- lengths: int32 [24], replicated, may hold values from 1 to 1152, 1536 in all
- mlp_owner: int32 [1536], replicated, may hold values from 0 to 7, as said below
- out_weight: bfloat16 [1024, 4096], P('tp'), may hold values from -0.1875 to 0.1875
- residual: bfloat16 [1536, 4096], P(('dc', 'tp')), may hold values from -3 to 3
Outputs:
- hidden: bfloat16 [1536, 4096], P(('dc', 'tp'))
Inputs may be any that keep to these rules, and one draw needn't show every extreme that they name: `mlp_owner`: the tokens of any one slab of 192 positions send at most 48 tokens to one owner, and every owner receives exactly 192 tokens.
All inputs are finite; a program needn't handle non-finite values.
Results may differ from a plain program's by a relative error of at most 0.013.
Values may be sent and summed in bfloat16 or wider, within the bound.
A program may use at most 128 MiB of HBM per device.

v0:
```python
import jax
import jax.numpy as jnp
from jax import lax
from jax.sharding import PartitionSpec as P

HEAD_SIZE = 128
GROUP = 4


neg_large = -1e30


def doc_index(positions, doc_ends):
    return jnp.sum((positions[:, None] >= doc_ends[None, :]).astype(jnp.int32), axis=1)


def mask_for(row_count, query_pos, query_doc, doc_ends):
    key_pos = jnp.arange(row_count, dtype=jnp.int32)
    key_doc = doc_index(key_pos, doc_ends)
    return (key_doc[None, :] == query_doc[:, None]) & (key_pos[None, :] <= query_pos[:, None])


def attend(running, key_piece, value_piece, allowed, query_heads):
    running_max, running_sum, accumulated = running
    scores = jnp.einsum(
        "qhd,kd->hqk", query_heads, key_piece, preferred_element_type=jnp.float32
    ) * HEAD_SIZE ** (-0.5)
    scores = jnp.where(allowed[None], scores, neg_large)
    new_max = jnp.maximum(running_max, jnp.max(scores, axis=2))
    weights = jnp.where(allowed[None], jnp.exp(scores - new_max[:, :, None]), 0.0)
    new_sum = jnp.sum(weights, axis=2)
    update = jnp.einsum(
        "hqk,kd->hqd", weights.astype(jnp.bfloat16), value_piece, preferred_element_type=jnp.float32
    )
    return (new_max, new_sum, update)


def per_device(queries, keys, values, lengths, mlp_owner, out_weight, residual):
    rows_here, columns = queries.shape
    heads_here = columns // HEAD_SIZE
    dc_count = lax.axis_size("dc")
    dc_index = lax.axis_index("dc")
    tp_index = lax.axis_index("tp")
    kv_group = tp_index * heads_here // GROUP
    key_head = lax.dynamic_slice_in_dim(keys, kv_group * HEAD_SIZE, HEAD_SIZE, 1)
    value_head = lax.dynamic_slice_in_dim(values, kv_group * HEAD_SIZE, HEAD_SIZE, 1)
    doc_ends = jnp.cumsum(lengths)
    local_rows = jnp.arange(rows_here, dtype=jnp.int32)
    query_pos = dc_index * rows_here + local_rows
    own_targets = lax.dynamic_slice_in_dim(mlp_owner, dc_index * rows_here, rows_here, 0)
    spread = 1
    query_doc = doc_index(query_pos, doc_ends)
    query_heads = queries.reshape(rows_here, heads_here, HEAD_SIZE)
    initial = (
        jnp.full((heads_here, rows_here), neg_large, jnp.float32),
        jnp.zeros((heads_here, rows_here), jnp.float32),
        jnp.zeros((heads_here, rows_here, HEAD_SIZE), jnp.float32),
    )
    key_piece = lax.all_gather(key_head, "dc", axis=0, tiled=True)
    value_piece = lax.all_gather(value_head, "dc", axis=0, tiled=True)
    allowed = mask_for(key_piece.shape[0], query_pos, query_doc, doc_ends)

    def compute():
        return attend(initial, key_piece, value_piece, allowed, query_heads)

    def unchanged():
        return initial

    outcome = lax.cond(jnp.any(allowed), compute, unchanged)
    running_max, running_sum, accumulated = outcome
    attention = (accumulated / running_sum[:, :, None]).astype(jnp.bfloat16)
    attention = jnp.transpose(attention, (1, 0, 2)).reshape(rows_here, columns)
    capacity = spread * ((rows_here + dc_count - 1) // dc_count + rows_here // dc_count)
    slot_total = dc_count * capacity
    earlier = local_rows[None, :] < local_rows[:, None]
    same_target = own_targets[None, :] == own_targets[:, None]
    slot_rank = jnp.sum((same_target & earlier).astype(jnp.int32), axis=1)
    slot_index = own_targets * capacity + slot_rank
    slot_ids = jnp.arange(slot_total, dtype=jnp.int32)
    placement = (slot_ids[:, None] == slot_index[None, :]).astype(jnp.bfloat16)
    outgoing = jnp.dot(placement, attention, preferred_element_type=jnp.float32).astype(
        jnp.bfloat16
    )
    outgoing = outgoing.reshape(dc_count, capacity, columns)
    incoming = lax.all_to_all(outgoing, "dc", split_axis=0, concat_axis=0, tiled=True)
    mine_blocks = (mlp_owner == dc_index).astype(jnp.bfloat16).reshape(dc_count, rows_here)
    lower_ones = (local_rows[:, None] <= local_rows[None, :]).astype(jnp.bfloat16)
    within_prefix = jnp.dot(mine_blocks, lower_ones, preferred_element_type=jnp.float32).astype(
        jnp.int32
    )
    block_counts = within_prefix[:, rows_here - 1]
    block_ids = jnp.arange(dc_count, dtype=jnp.int32)
    block_start = jnp.sum(
        jnp.where(block_ids[None, :] < block_ids[:, None], block_counts[None, :], 0), axis=1
    )
    mine_flat = mine_blocks.reshape(dc_count * rows_here) > 0
    rank_flat = (block_start[:, None] + within_prefix - 1).reshape(dc_count * rows_here)
    rank_flat = jnp.where(mine_flat, rank_flat, -1)
    all_pos = jnp.arange(dc_count * rows_here, dtype=jnp.int32)
    token_ids = jnp.sum(
        jnp.where(rank_flat[None, :] == local_rows[:, None], all_pos[None, :], 0), axis=1
    )
    token_slab = token_ids // rows_here
    token_within = token_ids % rows_here
    token_holder = jnp.where(token_within < rows_here, token_slab, dc_count - 1 - token_slab)
    same_holder = token_holder[None, :] == token_holder[:, None]
    before_here = token_within[None, :] < token_within[:, None]
    held_rank = jnp.sum((same_holder & before_here).astype(jnp.int32), axis=1)
    token_slots = token_holder * capacity + held_rank
    chooser = (token_slots[:, None] == slot_ids[None, :]).astype(jnp.bfloat16)
    incoming_flat = incoming.reshape(slot_total, columns)
    owned_rows = jnp.dot(chooser, incoming_flat, preferred_element_type=jnp.float32).astype(
        jnp.bfloat16
    )
    summed = lax.psum_scatter(
        jnp.dot(owned_rows, out_weight, preferred_element_type=jnp.float32).astype(jnp.bfloat16),
        "tp",
        scatter_dimension=0,
        tiled=True,
    ).astype(jnp.float32)
    return (summed + residual.astype(jnp.float32)).astype(jnp.bfloat16)


def solution(mesh):
    return jax.shard_map(
        per_device,
        mesh=mesh,
        in_specs=(
            P("dc", "tp"),
            P("dc", None),
            P("dc", None),
            P(),
            P(),
            P("tp", None),
            P(("dc", "tp"), None),
        ),
        out_specs=P(("dc", "tp"), None),
        check_vma=False,
    )
```

profile of v0, /device:TPU:0, one launch (start us, length us, event | category | flops | bytes accessed | tf_op | source)
XLA Modules:
  0.0 92.5 jit_solution(241320006936471670)
XLA Ops:
  6.5 1.0 %constant_dynamic-slice_fusion.1 = bf16[192,128]{1,0:T(8,128)(2,1)S(1)} fusion(bf16[192,256]{1,0:T(8,128)(2,1)} %param.10, s32[]{:T(128)S(6)} %select_n.92), kind=kLoop, calls=%fused_computation.55 | loop fusion | bytes 98308 | tf_op jit(solution)/shard_map/dynamic_slice | solution.py:45
  7.5 11.0 %all_gather.6 = bf16[1536,128]{1,0:T(8,128)(2,1)S(1)} all-gather(bf16[192,128]{1,0:T(8,128)(2,1)S(1)} %constant_dynamic-slice_fusion.1), channel_id=1, replica_groups=mesh['dc'=8,'tp'=4] {'dc'}, dimensions={0}, use_global_device_ids=true | all-gather | bytes 442368 | tf_op jit(solution)/shard_map/all_gather | solution.py:59
  18.5 0.8 constant_dynamic-slice_fusion
  19.3 9.5 %all_gather.7 = bf16[1536,128]{1,0:T(8,128)(2,1)S(1)} all-gather(bf16[192,128]{1,0:T(8,128)(2,1)S(1)} %constant_dynamic-slice_fusion), channel_id=1, replica_groups=mesh['dc'=8,'tp'=4] {'dc'}, dimensions={0}, use_global_device_ids=true | all-gather | bytes 442368 | tf_op jit(solution)/shard_map/all_gather | solution.py:60
  28.9 0.7 copy.15
  29.6 0.1 reduce.1
  29.8 0.1 convert_reduce_fusion.2
  29.9 0.1 convert_reduce_fusion.3
  30.0 1.0 %fusion.14 = (pred[192,1536]{1,0:T(8,128)(4,1)S(1)}, pred[]{:T(512)}) fusion(s32[192]{0:T(256)S(1)} %iota_add_fusion, s32[1536]{0:T(1024)S(1)} %convert_reduce_fusion.2, s32[192]{0:T(256)S(1)} %convert_reduce_fusion.3), kind=kLoop, calls=%fused_computation.20 | loop fusion | flops 1179647 | bytes 302593 | tf_op jit(solution)/shard_map/and | solution.py:20
  31.6 0.8 dynamic_slice.9
  32.4 0.2 convert_reduce_fusion
  32.6 0.8 multiply_add_fusion
  33.4 3.1 %conditional.1 = (f32[2,192]{1,0:T(2,128)S(1)}, f32[2,192,128]{2,1,0:T(8,128)S(1)}) conditional(s32[]{:T(128)} %convert_element_type.54, () %tuple.13, (pred[192,1536]{1,0:T(8,128)(4,1)S(1)}, bf16[192,256]{1,0:T(8,128)(2,1)}, bf16[1536,128]{1,0:T(8,128)(2,1)S(1)}, bf16[1536,128]{1,0:T(8,128)(2,1)S(1)}) %tuple.14), branch_computations={%region_8.9_spmd, %region_9.12_spmd} | conditional | flops 307297920 | bytes 9053200 | solution.py:69
  33.4 1.6 %fusion.23 = (f32[2,192]{1,0:T(2,128)S(1)}, f32[2,192,1536]{2,1,0:T(8,128)S(1)}) fusion(bf16[1536,128]{1,0:T(8,128)(2,1)S(1)} %get-tuple-element.15, pred[192,1536]{1,0:T(8,128)(4,1)S(1)} %get-tuple-element.14, bf16[192,256]{1,0:T(8,128)(2,1)} %get-tuple-element.23), kind=kOutput, calls=%fused_computation.57 | convolution fusion | flops 152764032 | bytes 3147264 | tf_op jit(solution)/shard_map/cond/branch_1_fun/qhd,kd->hqk/dot_general | solution.py:25
  35.0 0.7 fusion.4
  35.7 0.7 fusion.3
  36.4 1.0 %convolution_convert_fusion.1 = bf16[384,256]{1,0:T(8,128)(2,1)} fusion(s32[192]{0:T(256)S(1)} %multiply_add_fusion, f32[2,192,128]{2,1,0:T(8,128)S(1)} %get-tuple-element.20, f32[2,192]{1,0:T(2,128)S(1)} %get-tuple-element.21), kind=kOutput, calls=%fused_computation.21 | convolution fusion | flops 38019072 | bytes 395520 | tf_op jit(solution)/shard_map/dot_general | solution.py:81
  37.4 3.4 %all-to-all-start = ((bf16[8,48,256]{2,1,0:T(8,128)(2,1)}), bf16[8,48,256]{2,1,0:T(8,128)(2,1)S(1)}, u32[]{:S(2)}, u32[]{:S(2)}) async-start(bf16[8,48,256]{2,1,0:T(8,128)(2,1)} %bitcast.5), calls=%async_computation | async-start | bytes 393216 | tf_op jit(solution)/shard_map/all_to_all | solution.py:85
  40.8 0.0 reduce-scatter.2.cloned.1.call-start
  40.9 0.1 reshape.104
  41.0 0.1 convolution_convert_fusion.3
  41.1 0.2 slice_reduce_fusion
  41.3 0.1 select_reduce_fusion.1
  41.4 0.1 add_add_fusion
  41.5 0.1 reshape.105
  41.6 0.2 select_reduce_fusion
  41.8 0.2 convert_reduce_fusion.1
  42.1 4.9 %all-to-all-done = bf16[8,48,256]{2,1,0:T(8,128)(2,1)S(1)} async-done(((bf16[8,48,256]{2,1,0:T(8,128)(2,1)}), bf16[8,48,256]{2,1,0:T(8,128)(2,1)S(1)}, u32[]{:S(2)}, u32[]{:S(2)}) %all-to-all-start) | async-done | bytes 196640 | tf_op jit(solution)/shard_map/all_to_all | solution.py:85
  47.0 2.0 %convolution_convert_fusion = bf16[192,4096]{1,0:T(8,128)(2,1)} fusion(bf16[256,4096]{1,0:T(8,128)(2,1)S(1)} %copy-done, bf16[384,256]{1,0:T(8,128)(2,1)S(1)} %bitcast.35, s32[192]{0:T(256)S(1)} %multiply_add_fusion.1), kind=kOutput, calls=%fused_computation.16 | convolution fusion | flops 441311232 | bytes 3867392 | tf_op jit(solution)/shard_map/dot_general | solution.py:116
  49.0 0.0 reduce-scatter.2.cloned.1.call-update
  49.0 34.8 %reduce-scatter.2.cloned.1.call-done = bf16[48,4096]{1,0:T(8,128)(2,1)} async-done(((bf16[192,4096]{1,0:T(8,128)(2,1)}), bf16[48,4096]{1,0:T(8,128)(2,1)}) %reduce-scatter.2.cloned.1.call-update) | async-done | bytes 393232 | tf_op jit(solution)/shard_map/reduce_scatter | solution.py:115
  83.8 1.8 %add_convert_fusion = bf16[48,4096]{1,0:T(8,128)(2,1)} fusion(bf16[48,4096]{1,0:T(8,128)(2,1)S(1)} %copy-done.1, bf16[48,4096]{1,0:T(8,128)(2,1)} %reduce-scatter.2.cloned.1.call-done), kind=kLoop, calls=%fused_computation.24 | loop fusion | flops 786432 | bytes 1179648 | tf_op jit(solution)/shard_map/convert_element_type | solution.py:121
  (13 shorter events, 0.1 us)
Async XLA Ops:
  6.5 40.5 %copy-start = (bf16[256,4096]{1,0:T(8,128)(2,1)S(1)}, bf16[256,4096]{1,0:T(8,128)(2,1)}, u32[]{:S(2)}) copy-start(bf16[256,4096]{1,0:T(8,128)(2,1)} %param.14) | copy-start | bytes 6291460
  33.4 7.5 %copy-start.2 = (s32[1536]{0:T(1024)S(1)}, s32[1536]{0:T(1024)}, u32[]{:S(2)}) copy-start(s32[1536]{0:T(1024)} %param.13) | copy-start | bytes 18436
  37.4 9.6 %all-to-all-start = ((bf16[8,48,256]{2,1,0:T(8,128)(2,1)}), bf16[8,48,256]{2,1,0:T(8,128)(2,1)S(1)}, u32[]{:S(2)}, u32[]{:S(2)}) async-start(bf16[8,48,256]{2,1,0:T(8,128)(2,1)} %bitcast.5), calls=%async_computation | async-start | bytes 393216 | tf_op jit(solution)/shard_map/all_to_all | solution.py:85
  40.8 43.0 %reduce-scatter.2.cloned.1.call-start = ((), (), s32[]{:S(2)}) async-start(), calls=%async_computation.2 | async-start | bytes 1966080 | tf_op jit(solution)/shard_map/reduce_scatter | solution.py:115
  47.0 36.8 %copy-start.1 = (bf16[48,4096]{1,0:T(8,128)(2,1)S(1)}, bf16[48,4096]{1,0:T(8,128)(2,1)}, u32[]{:S(2)}) copy-start(bf16[48,4096]{1,0:T(8,128)(2,1)} %param.15) | copy-start | bytes 1179652
Sparse Core Ops, SparseCore 0:
  49.2 34.6 reduce-scatter.1
where the time goes:
time: 93 us; the launch traced here: 92.5 us
  waiting for transfers between devices  39.8 us (43%)
  blocking collectives  20.6 us (22%)
  between operations  14.1 us (15%)
  other arithmetic  5.57 us (6%)
  matrix products  5.45 us (6%)
  local copies, waits for them, and re-layouts  3.62 us (4%)
  starting transfers between devices  3.43 us (4%)
    reduce_scatter x1, waiting for transfers between devices, per_device(): lax.psum_scatter(jnp.dot(owned_rows, out_weight, preferred_element_type=j...  34.8 us
    all_gather x1, blocking collectives, per_device(): key_piece = lax.all_gather(key_head, 'dc', axis=0, tiled=True)  11 us
    all_gather x1, blocking collectives, per_device(): value_piece = lax.all_gather(value_head, 'dc', axis=0, tiled=True)  9.55 us
    all_to_all x1, waiting for transfers between devices, per_device(): lax.all_to_all(outgoing, 'dc', split_axis=0, concat_axis=0, tiled=True)  4.94 us
    all_to_all x1, starting transfers between devices, per_device(): lax.all_to_all(outgoing, 'dc', split_axis=0, concat_axis=0, tiled=True)  3.39 us
    dot_general x1, matrix products, per_device(): jnp.dot(owned_rows, out_weight, preferred_element_type=jnp.float32)  2.01 us
  transfers between devices with their start and end apart: 2, of which 2 were waited for; matrix products, arithmetic and copies ran while one was open for 1% of the time, Pallas kernels for 0%

commit v1 on v0

--- a/solution.py
+++ b/solution.py
@@ -1,6 +1,10 @@
+import functools
+
 import jax
 import jax.numpy as jnp
 from jax import lax
+from jax.experimental import pallas as pl
+from jax.experimental.pallas import tpu as pltpu
 from jax.sharding import PartitionSpec as P
 
 HEAD_SIZE = 128
@@ -44,7 +48,8 @@
     kv_group = tp_index * heads_here // GROUP
     key_head = lax.dynamic_slice_in_dim(keys, kv_group * HEAD_SIZE, HEAD_SIZE, 1)
     value_head = lax.dynamic_slice_in_dim(values, kv_group * HEAD_SIZE, HEAD_SIZE, 1)
-    doc_ends = jnp.cumsum(lengths)
+    order = jnp.arange(lengths.shape[0], dtype=jnp.int32)
+    doc_ends = jnp.sum(jnp.where(order[None, :] <= order[:, None], lengths[None, :], 0), axis=1)
     local_rows = jnp.arange(rows_here, dtype=jnp.int32)
     query_pos = dc_index * rows_here + local_rows
     own_targets = lax.dynamic_slice_in_dim(mlp_owner, dc_index * rows_here, rows_here, 0)
@@ -121,9 +126,259 @@
     return (summed + residual.astype(jnp.float32)).astype(jnp.bfloat16)
 
 
+MESH = pl.DeviceIdType.MESH
+SHARERS = 2
+COLUMN_CHUNK = 256
+
+
+def fused(dc_count, tp_count, lengths, owners, queries, keys, values, weight, out,
+          key_all, value_all, attn, outgoing, incoming, rows_all, weight_cols, finished,
+          kv_send, kv_recv, route_send, route_recv, share_send, share_recv,
+          weight_send, weight_recv, pass_send, pass_recv, own_sem, out_send, out_recv):
+    rows, columns = queries.shape
+    heads = columns // HEAD_SIZE
+    depth, width = weight.shape
+    my_width = width // tp_count
+    quarter = rows // tp_count
+    capacity = incoming.shape[0] // dc_count
+    total = dc_count * rows
+    part = depth // SHARERS
+    me, tp = lax.axis_index("dc"), lax.axis_index("tp")
+    group = tp * heads // GROUP
+    head_cols = pl.ds(pl.multiple_of(group * HEAD_SIZE, HEAD_SIZE), HEAD_SIZE)
+    lane = lax.rem(me, SHARERS)
+    base = me - lane
+
+    def remote(src, dst, send, recv, **where):
+        return pltpu.make_async_remote_copy(
+            src_ref=src, dst_ref=dst, send_sem=send, recv_sem=recv,
+            device_id=where, device_id_type=MESH)
+
+    barrier = pltpu.get_barrier_semaphore()
+    for o in range(1, dc_count):
+        pl.semaphore_signal(barrier, inc=1, device_id={"dc": lax.rem(me + o, dc_count)}, device_id_type=MESH)
+    for o in range(1, tp_count):
+        pl.semaphore_signal(barrier, inc=1, device_id={"tp": lax.rem(tp + o, tp_count)}, device_id_type=MESH)
+    pl.semaphore_wait(barrier, dc_count + tp_count - 2)
+
+    def kv_copies(o, slab, peer):
+        at = pl.ds(pl.multiple_of(slab * rows, rows), rows)
+        return (
+            remote(keys.at[:, head_cols], key_all.at[at], kv_send.at[o, 0], kv_recv.at[o, 0], dc=peer),
+            remote(values.at[:, head_cols], value_all.at[at], kv_send.at[o, 1], kv_recv.at[o, 1], dc=peer),
+        )
+
+    for o in range(1, dc_count):
+        @pl.when(me + o < dc_count)
+        def _():
+            for copy in kv_copies(o, me, me + o):
+                copy.start()
+
+    my_part = pl.ds(pl.multiple_of(lane * part, part), part)
+
+    def weight_copy(o, source, peer):
+        return remote(weight.at[my_part, pl.ds(pl.multiple_of(peer * my_width, my_width), my_width)],
+                      weight_cols.at[source, my_part], weight_send.at[o], weight_recv.at[o], tp=peer)
+
+    for o in range(1, tp_count):
+        weight_copy(o, tp, lax.rem(tp + o, tp_count)).start()
+    own = pltpu.make_async_copy(
+        weight.at[:, pl.ds(pl.multiple_of(tp * my_width, my_width), my_width)], weight_cols.at[tp], own_sem)
+    own.start()
+
+    mine = pl.ds(pl.multiple_of(me * rows, rows), rows)
+    key_all[mine, :] = keys[:, head_cols]
+    value_all[mine, :] = values[:, head_cols]
+    for o in range(1, dc_count):
+        @pl.when(me + o < dc_count)
+        def _():
+            later = pl.ds(pl.multiple_of((me + o) * rows, rows), rows)
+            key_all[later, :] = jnp.zeros((rows, HEAD_SIZE), key_all.dtype)
+            value_all[later, :] = jnp.zeros((rows, HEAD_SIZE), value_all.dtype)
+
+    position = me * rows + lax.broadcasted_iota(jnp.int32, (rows, 1), 0)
+    first = jnp.zeros((rows, 1), jnp.int32)
+    end = jnp.int32(0)
+    for k in range(lengths.shape[0]):
+        end = end + lengths[k]
+        first = jnp.where(position >= end, end, first)
+
+    my_targets = owners[pl.ds(me, 1), :]
+    hot = (lax.broadcasted_iota(jnp.int32, (dc_count, rows), 0) == my_targets)
+    before = (lax.broadcasted_iota(jnp.int32, (rows, rows), 0)
+              < lax.broadcasted_iota(jnp.int32, (rows, rows), 1)).astype(jnp.float32).astype(jnp.bfloat16)
+    hot_f = hot.astype(jnp.float32)
+    prefix = jnp.dot(hot_f.astype(jnp.bfloat16), before, preferred_element_type=jnp.float32)
+    rank = jnp.sum(hot_f * prefix, axis=0, keepdims=True)
+    slot = my_targets.astype(jnp.float32) * capacity + rank
+    slot_ids = lax.broadcasted_iota(jnp.int32, (dc_count * capacity, rows), 0).astype(jnp.float32)
+    placement = jnp.where(slot_ids == slot, 1.0, 0.0).astype(jnp.bfloat16)
+
+    counts = jnp.sum((owners[...] == me).astype(jnp.float32), axis=1, keepdims=True)
+    slots = lax.broadcasted_iota(jnp.int32, (1, dc_count * capacity), 1).astype(jnp.float32)
+    goal = jnp.full((1, dc_count * capacity), -1.0, jnp.float32)
+    begin = jnp.zeros((1, 1), jnp.float32)
+    for s in range(dc_count):
+        held = counts[s : s + 1, :]
+        k = slots - float(s * capacity)
+        goal = jnp.where((k >= 0.0) & (k < held), begin + k, goal)
+        begin = begin + held
+    out_rows = lax.broadcasted_iota(jnp.int32, (rows, dc_count * capacity), 0).astype(jnp.float32)
+    chooser = jnp.where(out_rows == goal, 1.0, 0.0).astype(jnp.bfloat16)
+
+    for o in range(1, dc_count):
+        @pl.when(me - o >= 0)
+        def _():
+            for copy in kv_copies(o, me - o, me):
+                copy.wait_recv()
+
+    key_pos = lax.broadcasted_iota(jnp.int32, (rows, total), 1)
+    allowed = (key_pos >= first) & (key_pos <= position)
+    for h in range(heads):
+        cols = slice(h * HEAD_SIZE, (h + 1) * HEAD_SIZE)
+        scores = lax.dot_general(queries[:, cols], key_all[...], (((1,), (1,)), ((), ())),
+                                 preferred_element_type=jnp.float32) * HEAD_SIZE ** (-0.5)
+        scores = jnp.where(allowed, scores, neg_large)
+        weights = jnp.exp(scores - jnp.max(scores, axis=1, keepdims=True))
+        weights = jnp.where(allowed, weights, 0.0)
+        mixed = jnp.dot(weights.astype(jnp.bfloat16), value_all[...], preferred_element_type=jnp.float32)
+        attn[:, cols] = (mixed / jnp.sum(weights, axis=1, keepdims=True)).astype(attn.dtype)
+
+    outgoing[...] = jnp.dot(placement, attn[...], preferred_element_type=jnp.float32).astype(outgoing.dtype)
+
+    def route_copy(o, source, peer):
+        return remote(outgoing.at[pl.ds(pl.multiple_of(peer * capacity, capacity), capacity)],
+                      incoming.at[pl.ds(pl.multiple_of(source * capacity, capacity), capacity)],
+                      route_send.at[o], route_recv.at[o], dc=peer)
+
+    for o in range(1, dc_count):
+        route_copy(o, me, lax.rem(me + o, dc_count)).start()
+    here = pl.ds(pl.multiple_of(me * capacity, capacity), capacity)
+    incoming[here, :] = outgoing[here, :]
+
+    def pass_copy(o, p, source, rows_at, peer):
+        return remote(weight_cols.at[source, rows_at], weight_cols.at[source, rows_at],
+                      pass_send.at[o, p], pass_recv.at[o, p], dc=peer)
+
+    def pass_on(o):
+        source = lax.rem(tp - o + tp_count, tp_count)
+        weight_copy(o, source, tp).wait_recv()
+        for p in range(1, SHARERS):
+            pass_copy(o, p, source, my_part, base + lax.rem(lane + p, SHARERS)).start()
+
+    for o in range(1, dc_count):
+        route_copy(o, lax.rem(me - o + dc_count, dc_count), me).wait_recv()
+    rows_all[tp] = jnp.dot(chooser, incoming[...], preferred_element_type=jnp.float32).astype(rows_all.dtype)
+
+    def share_copy(o, source, peer):
+        return remote(rows_all.at[source], rows_all.at[source], share_send.at[o], share_recv.at[o], tp=peer)
+
+    for o in range(1, tp_count):
+        share_copy(o, tp, lax.rem(tp + o, tp_count)).start()
+    for o in range(1, tp_count):
+        pass_on(o)
+    own.wait()
+    for o in range(1, tp_count):
+        source = lax.rem(tp - o + tp_count, tp_count)
+        share_copy(o, source, tp).wait_recv()
+        for p in range(1, SHARERS):
+            theirs = lax.rem(lane - p + SHARERS, SHARERS)
+            at = pl.ds(pl.multiple_of(theirs * part, part), part)
+            pass_copy(o, p, source, at, me).wait_recv()
+
+    def out_copy(o, c, source, peer):
+        return remote(finished.at[pl.ds(pl.multiple_of(peer * quarter, quarter), quarter),
+                                  c * COLUMN_CHUNK : (c + 1) * COLUMN_CHUNK],
+                      out.at[:, pl.ds(pl.multiple_of(source * my_width + c * COLUMN_CHUNK, COLUMN_CHUNK), COLUMN_CHUNK)],
+                      out_send.at[o, c], out_recv.at[o, c], tp=peer)
+
+    chunks = my_width // COLUMN_CHUNK
+    for c in range(chunks):
+        cols = slice(c * COLUMN_CHUNK, (c + 1) * COLUMN_CHUNK)
+        acc = jnp.dot(rows_all[0], weight_cols[0, :, cols], preferred_element_type=jnp.float32)
+        for r in range(1, tp_count):
+            acc = acc + jnp.dot(rows_all[r], weight_cols[r, :, cols], preferred_element_type=jnp.float32)
+        finished[:, cols] = acc.astype(finished.dtype)
+        for o in range(1, tp_count):
+            out_copy(o, c, tp, lax.rem(tp + o, tp_count)).start()
+    keep = finished[pl.ds(pl.multiple_of(tp * quarter, quarter), quarter), :]
+    out[:, pl.ds(pl.multiple_of(tp * my_width, my_width), my_width)] = keep
+
+    for o in range(1, tp_count):
+        for c in range(chunks):
+            out_copy(o, c, lax.rem(tp - o + tp_count, tp_count), tp).wait_recv()
+    for o in range(1, dc_count):
+        @pl.when(me + o < dc_count)
+        def _():
+            for copy in kv_copies(o, me, me + o):
+                copy.wait_send()
+        route_copy(o, me, lax.rem(me + o, dc_count)).wait_send()
+    for o in range(1, tp_count):
+        peer = lax.rem(tp + o, tp_count)
+        weight_copy(o, tp, peer).wait_send()
+        share_copy(o, tp, peer).wait_send()
+        for p in range(1, SHARERS):
+            pass_copy(o, p, lax.rem(tp - o + tp_count, tp_count), my_part,
+                      base + lax.rem(lane + p, SHARERS)).wait_send()
+        for c in range(chunks):
+            out_copy(o, c, tp, peer).wait_send()
+
+
+def in_one_kernel(dc_count, tp_count, queries, keys, values, lengths, mlp_owner, out_weight, residual):
+    rows, columns = queries.shape
+    depth, width = out_weight.shape
+    capacity = (rows + dc_count - 1) // dc_count + rows // dc_count
+    chunks = width // tp_count // COLUMN_CHUNK
+    half = jnp.bfloat16
+    dma = pltpu.SemaphoreType.DMA
+    vmem, smem = pl.BlockSpec(memory_space=pltpu.VMEM), pl.BlockSpec(memory_space=pltpu.SMEM)
+    summed = pl.pallas_call(
+        functools.partial(fused, dc_count, tp_count),
+        out_shape=jax.ShapeDtypeStruct((rows // tp_count, width), half),
+        in_specs=[smem, vmem, vmem, vmem, vmem, pl.BlockSpec(memory_space=pl.ANY)],
+        out_specs=vmem,
+        scratch_shapes=[
+            pltpu.VMEM((dc_count * rows, HEAD_SIZE), half),
+            pltpu.VMEM((dc_count * rows, HEAD_SIZE), half),
+            pltpu.VMEM((rows, columns), half),
+            pltpu.VMEM((dc_count * capacity, columns), half),
+            pltpu.VMEM((dc_count * capacity, columns), half),
+            pltpu.VMEM((tp_count, rows, columns), half),
+            pltpu.VMEM((tp_count, depth, width // tp_count), half),
+            pltpu.VMEM((rows, width // tp_count), half),
+            dma((dc_count, 2)), dma((dc_count, 2)),
+            dma((dc_count,)), dma((dc_count,)),
+            dma((tp_count,)), dma((tp_count,)),
+            dma((tp_count,)), dma((tp_count,)),
+            dma((tp_count, SHARERS)), dma((tp_count, SHARERS)),
+            dma(()),
+            dma((tp_count, chunks)), dma((tp_count, chunks)),
+        ],
+        compiler_params=pltpu.CompilerParams(
+            collective_id=0, has_side_effects=True, vmem_limit_bytes=40 * 2**20),
+    )(lengths, mlp_owner.reshape(dc_count, rows), queries, keys, values, out_weight)
+    return (summed.astype(jnp.float32) + residual.astype(jnp.float32)).astype(half)
+
+
+def body(dc_count, tp_count, *arrays):
+    queries, out_weight = arrays[0], arrays[5]
+    rows, width = queries.shape[0], out_weight.shape[1]
+    fits = (
+        width % (tp_count * COLUMN_CHUNK) == 0
+        and dc_count % SHARERS == 0
+        and rows % (16 * tp_count) == 0
+        and rows // dc_count * dc_count == rows
+        and (2 * (rows // dc_count)) % 16 == 0
+        and dc_count * rows <= 2048
+    )
+    if fits:
+        return in_one_kernel(dc_count, tp_count, *arrays)
+    return per_device(*arrays)
+
+
 def solution(mesh):
     return jax.shard_map(
-        per_device,
+        functools.partial(body, mesh.shape["dc"], mesh.shape["tp"]),
         mesh=mesh,
         in_specs=(
             P("dc", "tp"),

time: 93 us -> 55.1 us (0.59)
  Pallas kernels: 0 us -> 48.3 us
  waiting for transfers between devices: 39.8 us -> 0 us
  blocking collectives: 20.6 us -> 0 us
  between operations: 14.1 us -> 0.02 us
  matrix products: 5.45 us -> 0 us
  other arithmetic: 5.57 us -> 0.84 us
  starting transfers between devices: 3.43 us -> 0 us
  local copies, waits for them, and re-layouts: 3.62 us -> 5.69 us
    pallas_call x0 -> x1, Pallas kernels: none -> 48.3 us  [in_one_kernel(): pl.pallas_call(functools.partial(fused, dc_count, tp_count), out_shape=ja...]
    reduce_scatter x1 -> x0, waiting for transfers between devices: 34.8 us -> none  [per_device(): lax.psum_scatter(jnp.dot(owned_rows, out_weight, preferred_element_type=j...]
    all_gather x2 -> x0, blocking collectives: 20.6 us -> none  [the longest x1 11 us: per_device(): key_piece = lax.all_gather(key_head, 'dc', axis=0, tiled=True)]
    dot_general x5 -> x0, matrix products: 5.45 us -> none  [the longest x1 2.01 us: per_device(): jnp.dot(owned_rows, out_weight, preferred_element_type=jnp.float32)]
    all_to_all x1 -> x0, waiting for transfers between devices: 4.94 us -> none  [per_device(): lax.all_to_all(outgoing, 'dc', split_axis=0, concat_axis=0, tiled=True)]
    unnamed x6 -> x12, local copies, waits for them, and re-layouts: 0.01 us -> 4.93 us
    all_to_all x1 -> x0, starting transfers between devices: 3.39 us -> none  [per_device(): lax.all_to_all(outgoing, 'dc', split_axis=0, concat_axis=0, tiled=True)]
    dynamic_slice x3 -> x0, local copies, waits for them, and re-layouts: 2.53 us -> none  [the longest x1 0.95 us: per_device(): lax.dynamic_slice_in_dim(keys, kv_group * HEAD_SIZE, HEAD_SIZE, 1)]
  transfers between devices with their start and end apart: 2 -> 0, of which waited for: 2 -> 0; matrix products, arithmetic and copies ran while one was open for 1% -> 0% of each run, Pallas kernels for 0% -> 0%
where the time goes in v1:
time: 55.1 us; the launch traced here: 54.8 us
  Pallas kernels  48.3 us (88%)
  local copies, waits for them, and re-layouts  5.69 us (10%)
  other arithmetic  0.84 us (2%)
    pallas_call x1, Pallas kernels, in_one_kernel(): pl.pallas_call(functools.partial(fused, dc_count, tp_count), out_shape=ja...  48.3 us
    unnamed x12, local copies, waits for them, and re-layouts  4.93 us

profile of v1, /device:TPU:0, one launch (start us, length us, event | category | flops | bytes accessed | tf_op | source)
XLA Modules:
  0.0 54.8 jit_solution(5703970731486090633)
XLA Ops:
  0.0 0.8 %reshape.3.owners = s32[8,192]{1,0:T(8,128)S(1)} reshape(s32[1536]{0:T(1024)} %param.11) | data formatting | bytes 12288 | tf_op jit(solution)/shard_map/reshape | solution.py:359
  0.8 0.0 copy-start
  0.8 1.6 %copy-done = bf16[256,4096]{1,0:T(8,128)(2,1)S(1)} copy-done((bf16[256,4096]{1,0:T(8,128)(2,1)S(1)}, bf16[256,4096]{1,0:T(8,128)(2,1)}, u32[]{:S(2)}) %copy-start) | copy-done | bytes 2097176
  2.4 0.0 copy-start.1
  2.4 0.9 %copy-done.1 = bf16[192,256]{1,0:T(8,128)(2,1)S(1)} copy-done((bf16[192,256]{1,0:T(8,128)(2,1)S(1)}, bf16[192,256]{1,0:T(8,128)(2,1)}, u32[]{:S(2)}) %copy-start.1) | copy-done | bytes 98328
  3.3 0.0 copy-start.2
  3.3 0.9 %copy-done.2 = bf16[192,256]{1,0:T(8,128)(2,1)S(1)} copy-done((bf16[192,256]{1,0:T(8,128)(2,1)S(1)}, bf16[192,256]{1,0:T(8,128)(2,1)}, u32[]{:S(2)}) %copy-start.2) | copy-done | bytes 98328
  4.1 0.0 copy-start.3
  4.1 0.9 %copy-done.3 = bf16[192,256]{1,0:T(8,128)(2,1)S(1)} copy-done((bf16[192,256]{1,0:T(8,128)(2,1)S(1)}, bf16[192,256]{1,0:T(8,128)(2,1)}, u32[]{:S(2)}) %copy-start.3) | copy-done | bytes 98328
  5.0 0.0 copy-start.4
  5.0 0.7 %copy-done.4 = s32[24]{0:T(128)S(1)} copy-done((s32[24]{0:T(128)S(1)}, s32[24]{0:T(128)}, u32[]{:S(2)}) %copy-start.4) | copy-done | bytes 120
  5.7 0.0 copy-start.5
  5.7 48.3 %shard_map.73 = bf16[48,4096]{1,0:T(8,128)(2,1)S(1)} custom-call(s32[24]{0:T(128)S(1)} %copy-done.4, s32[8,192]{1,0:T(8,128)S(1)} %reshape.3.owners, bf16[192,256]{1,0:T(8,128)(2,1)S(1)} %copy-done.1, bf16[192,256]{1,0:T(8,128)(2,1)S(1)} %copy-done.2, bf16[192,256]{1,0:T(8,128)(2,1)S(1)} %copy-done.3, bf16[256,4096]{1,0:T(8,128)(2,1)S(1)} %copy-done), custom_call_target="tpu_custom_call" | custom-call | tf_op jit(solution)/shard_map/pallas_call | solution.py:335
  54.0 0.0 copy-done.5
  54.0 0.8 %add_convert_fusion = bf16[48,4096]{1,0:T(8,128)(2,1)} fusion(bf16[48,4096]{1,0:T(8,128)(2,1)S(1)} %copy-done.5, bf16[48,4096]{1,0:T(8,128)(2,1)S(1)} %shard_map.73), kind=kLoop, calls=%fused_computation | loop fusion | flops 786432 | bytes 1179648 | tf_op jit(solution)/shard_map/convert_element_type | solution.py:360
Async XLA Ops:
  0.8 1.6 %copy-start = (bf16[256,4096]{1,0:T(8,128)(2,1)S(1)}, bf16[256,4096]{1,0:T(8,128)(2,1)}, u32[]{:S(2)}) copy-start(bf16[256,4096]{1,0:T(8,128)(2,1)} %weight.1) | copy-start | bytes 6291460
  2.4 0.9 %copy-start.1 = (bf16[192,256]{1,0:T(8,128)(2,1)S(1)}, bf16[192,256]{1,0:T(8,128)(2,1)}, u32[]{:S(2)}) copy-start(bf16[192,256]{1,0:T(8,128)(2,1)} %queries.1) | copy-start | bytes 294916
  3.3 0.9 %copy-start.2 = (bf16[192,256]{1,0:T(8,128)(2,1)S(1)}, bf16[192,256]{1,0:T(8,128)(2,1)}, u32[]{:S(2)}) copy-start(bf16[192,256]{1,0:T(8,128)(2,1)} %keys.1) | copy-start | bytes 294916
  4.1 0.9 %copy-start.3 = (bf16[192,256]{1,0:T(8,128)(2,1)S(1)}, bf16[192,256]{1,0:T(8,128)(2,1)}, u32[]{:S(2)}) copy-start(bf16[192,256]{1,0:T(8,128)(2,1)} %values.1) | copy-start | bytes 294916
  5.0 0.7 %copy-start.4 = (s32[24]{0:T(128)S(1)}, s32[24]{0:T(128)}, u32[]{:S(2)}) copy-start(s32[24]{0:T(128)} %lengths.1) | copy-start | bytes 292
  5.7 48.3 %copy-start.5 = (bf16[48,4096]{1,0:T(8,128)(2,1)S(1)}, bf16[48,4096]{1,0:T(8,128)(2,1)}, u32[]{:S(2)}) copy-start(bf16[48,4096]{1,0:T(8,128)(2,1)} %param.13) | copy-start | bytes 1179652

commit v2 on v1

--- a/solution.py
+++ b/solution.py
@@ -127,33 +127,43 @@
 
 
 MESH = pl.DeviceIdType.MESH
-SHARERS = 2
+SHARERS = 4
 COLUMN_CHUNK = 256
 
 
 def fused(dc_count, tp_count, lengths, owners, queries, keys, values, weight, out,
-          key_all, value_all, attn, outgoing, incoming, rows_all, weight_cols, finished,
-          kv_send, kv_recv, route_send, route_recv, share_send, share_recv,
-          weight_send, weight_recv, pass_send, pass_recv, own_sem, out_send, out_recv):
+          query_own, kv_all, attn, outgoing, incoming, rows_all, weight_cols, finished,
+          kv_send, kv_recv, hand_send, hand_recv, pair_send, pair_recv, route_send, route_recv, share_send, share_recv,
+          weight_send, weight_recv, pass_send, pass_recv, own_sem, local_sem, out_send, out_recv):
     rows, columns = queries.shape
     heads = columns // HEAD_SIZE
     depth, width = weight.shape
     my_width = width // tp_count
     quarter = rows // tp_count
-    capacity = incoming.shape[0] // dc_count
+    capacity = incoming.shape[1] // dc_count
     total = dc_count * rows
     part = depth // SHARERS
     me, tp = lax.axis_index("dc"), lax.axis_index("tp")
     group = tp * heads // GROUP
     head_cols = pl.ds(pl.multiple_of(group * HEAD_SIZE, HEAD_SIZE), HEAD_SIZE)
-    lane = lax.rem(me, SHARERS)
-    base = me - lane
 
     def remote(src, dst, send, recv, **where):
         return pltpu.make_async_remote_copy(
             src_ref=src, dst_ref=dst, send_sem=send, recv_sem=recv,
             device_id=where, device_id_type=MESH)
 
+    mine = pl.ds(pl.multiple_of(me * rows, rows), rows)
+    local = (
+        pltpu.make_async_copy(keys.at[:, head_cols], kv_all.at[0, mine], local_sem.at[0]),
+        pltpu.make_async_copy(values.at[:, head_cols], kv_all.at[1, mine], local_sem.at[1]),
+        pltpu.make_async_copy(queries, query_own, local_sem.at[2]),
+    )
+    for copy in local:
+        copy.start()
+    own = pltpu.make_async_copy(
+        weight.at[:, pl.ds(pl.multiple_of(tp * my_width, my_width), my_width)], weight_cols.at[tp], own_sem)
+    own.start()
+
     barrier = pltpu.get_barrier_semaphore()
     for o in range(1, dc_count):
         pl.semaphore_signal(barrier, inc=1, device_id={"dc": lax.rem(me + o, dc_count)}, device_id_type=MESH)
@@ -161,40 +171,62 @@
         pl.semaphore_signal(barrier, inc=1, device_id={"tp": lax.rem(tp + o, tp_count)}, device_id_type=MESH)
     pl.semaphore_wait(barrier, dc_count + tp_count - 2)
 
-    def kv_copies(o, slab, peer):
-        at = pl.ds(pl.multiple_of(slab * rows, rows), rows)
-        return (
-            remote(keys.at[:, head_cols], key_all.at[at], kv_send.at[o, 0], kv_recv.at[o, 0], dc=peer),
-            remote(values.at[:, head_cols], value_all.at[at], kv_send.at[o, 1], kv_recv.at[o, 1], dc=peer),
-        )
-
+    for copy in local:
+        copy.wait()
+    core = lax.rem(me, 2)
+    pair = me - core
+    other = pair + 1 - core
+
+    def slab(index):
+        return pl.ds(pl.multiple_of(index * rows, rows), rows)
+
+    def kv_copy(first_of_pair, z, source):
+        block = kv_all.at[z, slab(source)]
+        return remote(block, block, kv_send.at[first_of_pair // 2, z], kv_recv.at[source], dc=first_of_pair + z)
+
+    def pair_copy(z, source, peer):
+        block = kv_all.at[z, slab(source)]
+        return remote(block, block, pair_send.at[z], pair_recv.at[z], dc=peer)
+
+    def hand_copy(z, source, peer):
+        block = kv_all.at[z, slab(source)]
+        return remote(block, block, hand_send.at[source], hand_recv.at[source], dc=peer)
+
+    for p in range(2, dc_count, 2):
+        @pl.when(pair < p)
+        def _():
+            for z in range(2):
+                kv_copy(p, z, me).start()
+
+    @pl.when(core == 0)
+    def _():
+        for z in range(2):
+            pair_copy(z, me, me + 1).start()
+
+    def sharing(o):
+        stride = 2 if o % 2 == 1 else dc_count // 2
+        bit = lax.rem(me // stride, 2)
+        return core + 2 * bit, me - core - bit * stride, stride
+
+    def part_of(lane):
+        return pl.ds(pl.multiple_of(lane * part, part), part)
+
+    def sharer(o, p):
+        lane, origin, stride = sharing(o)
+        there = lax.rem(lane + p, SHARERS)
+        return origin + lax.rem(there, 2) + there // 2 * stride
+
+    def weight_copy(o, source, peer):
+        return remote(weight.at[part_of(sharing(o)[0]), pl.ds(pl.multiple_of(peer * my_width, my_width), my_width)],
+                      weight_cols.at[source, part_of(sharing(o)[0])], weight_send.at[o], weight_recv.at[o], tp=peer)
+
+    for o in range(1, tp_count):
+        weight_copy(o, tp, lax.rem(tp + o, tp_count)).start()
     for o in range(1, dc_count):
         @pl.when(me + o < dc_count)
         def _():
-            for copy in kv_copies(o, me, me + o):
-                copy.start()
-
-    my_part = pl.ds(pl.multiple_of(lane * part, part), part)
-
-    def weight_copy(o, source, peer):
-        return remote(weight.at[my_part, pl.ds(pl.multiple_of(peer * my_width, my_width), my_width)],
-                      weight_cols.at[source, my_part], weight_send.at[o], weight_recv.at[o], tp=peer)
-
-    for o in range(1, tp_count):
-        weight_copy(o, tp, lax.rem(tp + o, tp_count)).start()
-    own = pltpu.make_async_copy(
-        weight.at[:, pl.ds(pl.multiple_of(tp * my_width, my_width), my_width)], weight_cols.at[tp], own_sem)
-    own.start()
-
-    mine = pl.ds(pl.multiple_of(me * rows, rows), rows)
-    key_all[mine, :] = keys[:, head_cols]
-    value_all[mine, :] = values[:, head_cols]
-    for o in range(1, dc_count):
-        @pl.when(me + o < dc_count)
-        def _():
-            later = pl.ds(pl.multiple_of((me + o) * rows, rows), rows)
-            key_all[later, :] = jnp.zeros((rows, HEAD_SIZE), key_all.dtype)
-            value_all[later, :] = jnp.zeros((rows, HEAD_SIZE), value_all.dtype)
+            for z in range(2):
+                kv_all[z, slab(me + o), :] = jnp.zeros((rows, HEAD_SIZE), kv_all.dtype)
 
     position = me * rows + lax.broadcasted_iota(jnp.int32, (rows, 1), 0)
     first = jnp.zeros((rows, 1), jnp.int32)
@@ -226,65 +258,74 @@
     out_rows = lax.broadcasted_iota(jnp.int32, (rows, dc_count * capacity), 0).astype(jnp.float32)
     chooser = jnp.where(out_rows == goal, 1.0, 0.0).astype(jnp.bfloat16)
 
-    for o in range(1, dc_count):
-        @pl.when(me - o >= 0)
-        def _():
-            for copy in kv_copies(o, me - o, me):
-                copy.wait_recv()
+    for source in range(dc_count - 2):
+        @pl.when(source < pair)
+        def _():
+            kv_copy(0, core, source).wait_recv()
+            hand_copy(core, source, other).start()
+
+    @pl.when(core == 1)
+    def _():
+        for z in range(2):
+            pair_copy(z, pair, me).wait_recv()
+
+    for source in range(dc_count - 2):
+        @pl.when(source < pair)
+        def _():
+            hand_copy(1 - core, source, me).wait_recv()
+
+    def pass_copy(o, p, source, rows_at, peer):
+        return remote(weight_cols.at[source, rows_at], weight_cols.at[source, rows_at],
+                      pass_send.at[o, p], pass_recv.at[o, p], dc=peer)
+
+    def pass_on(o):
+        source = lax.rem(tp - o + tp_count, tp_count)
+        weight_copy(o, source, tp).wait_recv()
+        for p in range(1, SHARERS):
+            pass_copy(o, p, source, part_of(sharing(o)[0]), sharer(o, p)).start()
+
+    def route_copy(o, h, source, peer):
+        return remote(outgoing.at[h, pl.ds(pl.multiple_of(peer * capacity, capacity), capacity)],
+                      incoming.at[h, pl.ds(pl.multiple_of(source * capacity, capacity), capacity)],
+                      route_send.at[o, h], route_recv.at[o, h], dc=peer)
+
+    def share_copy(o, h, source, peer):
+        return remote(rows_all.at[source, h], rows_all.at[source, h], share_send.at[o, h], share_recv.at[o, h], tp=peer)
 
     key_pos = lax.broadcasted_iota(jnp.int32, (rows, total), 1)
     allowed = (key_pos >= first) & (key_pos <= position)
     for h in range(heads):
         cols = slice(h * HEAD_SIZE, (h + 1) * HEAD_SIZE)
-        scores = lax.dot_general(queries[:, cols], key_all[...], (((1,), (1,)), ((), ())),
+        scores = lax.dot_general(query_own[:, cols], kv_all[0], (((1,), (1,)), ((), ())),
                                  preferred_element_type=jnp.float32) * HEAD_SIZE ** (-0.5)
         scores = jnp.where(allowed, scores, neg_large)
         weights = jnp.exp(scores - jnp.max(scores, axis=1, keepdims=True))
         weights = jnp.where(allowed, weights, 0.0)
-        mixed = jnp.dot(weights.astype(jnp.bfloat16), value_all[...], preferred_element_type=jnp.float32)
-        attn[:, cols] = (mixed / jnp.sum(weights, axis=1, keepdims=True)).astype(attn.dtype)
-
-    outgoing[...] = jnp.dot(placement, attn[...], preferred_element_type=jnp.float32).astype(outgoing.dtype)
-
-    def route_copy(o, source, peer):
-        return remote(outgoing.at[pl.ds(pl.multiple_of(peer * capacity, capacity), capacity)],
-                      incoming.at[pl.ds(pl.multiple_of(source * capacity, capacity), capacity)],
-                      route_send.at[o], route_recv.at[o], dc=peer)
-
-    for o in range(1, dc_count):
-        route_copy(o, me, lax.rem(me + o, dc_count)).start()
-    here = pl.ds(pl.multiple_of(me * capacity, capacity), capacity)
-    incoming[here, :] = outgoing[here, :]
-
-    def pass_copy(o, p, source, rows_at, peer):
-        return remote(weight_cols.at[source, rows_at], weight_cols.at[source, rows_at],
-                      pass_send.at[o, p], pass_recv.at[o, p], dc=peer)
-
-    def pass_on(o):
+        mixed = jnp.dot(weights.astype(jnp.bfloat16), kv_all[1], preferred_element_type=jnp.float32)
+        attn[h] = (mixed / jnp.sum(weights, axis=1, keepdims=True)).astype(attn.dtype)
+        outgoing[h] = jnp.dot(placement, attn[h], preferred_element_type=jnp.float32).astype(outgoing.dtype)
+        for o in range(1, dc_count):
+            route_copy(o, h, me, lax.rem(me + o, dc_count)).start()
+        here = pl.ds(pl.multiple_of(me * capacity, capacity), capacity)
+        incoming[h, here, :] = outgoing[h, here, :]
+
+    for o in range(1, tp_count):
+        pass_on(o)
+
+    for h in range(heads):
+        for o in range(1, dc_count):
+            route_copy(o, h, lax.rem(me - o + dc_count, dc_count), me).wait_recv()
+        rows_all[tp, h] = jnp.dot(chooser, incoming[h], preferred_element_type=jnp.float32).astype(rows_all.dtype)
+        for o in range(1, tp_count):
+            share_copy(o, h, tp, lax.rem(tp + o, tp_count)).start()
+    own.wait()
+    for o in range(1, tp_count):
         source = lax.rem(tp - o + tp_count, tp_count)
-        weight_copy(o, source, tp).wait_recv()
+        for h in range(heads):
+            share_copy(o, h, source, tp).wait_recv()
         for p in range(1, SHARERS):
-            pass_copy(o, p, source, my_part, base + lax.rem(lane + p, SHARERS)).start()
-
-    for o in range(1, dc_count):
-        route_copy(o, lax.rem(me - o + dc_count, dc_count), me).wait_recv()
-    rows_all[tp] = jnp.dot(chooser, incoming[...], preferred_element_type=jnp.float32).astype(rows_all.dtype)
-
-    def share_copy(o, source, peer):
-        return remote(rows_all.at[source], rows_all.at[source], share_send.at[o], share_recv.at[o], tp=peer)
-
-    for o in range(1, tp_count):
-        share_copy(o, tp, lax.rem(tp + o, tp_count)).start()
-    for o in range(1, tp_count):
-        pass_on(o)
-    own.wait()
-    for o in range(1, tp_count):
-        source = lax.rem(tp - o + tp_count, tp_count)
-        share_copy(o, source, tp).wait_recv()
-        for p in range(1, SHARERS):
-            theirs = lax.rem(lane - p + SHARERS, SHARERS)
-            at = pl.ds(pl.multiple_of(theirs * part, part), part)
-            pass_copy(o, p, source, at, me).wait_recv()
+            theirs = lax.rem(sharing(o)[0] - p + SHARERS, SHARERS)
+            pass_copy(o, p, source, part_of(theirs), me).wait_recv()
 
     def out_copy(o, c, source, peer):
         return remote(finished.at[pl.ds(pl.multiple_of(peer * quarter, quarter), quarter),
@@ -295,9 +336,10 @@
     chunks = my_width // COLUMN_CHUNK
     for c in range(chunks):
         cols = slice(c * COLUMN_CHUNK, (c + 1) * COLUMN_CHUNK)
-        acc = jnp.dot(rows_all[0], weight_cols[0, :, cols], preferred_element_type=jnp.float32)
-        for r in range(1, tp_count):
-            acc = acc + jnp.dot(rows_all[r], weight_cols[r, :, cols], preferred_element_type=jnp.float32)
+        acc = jnp.zeros((rows, COLUMN_CHUNK), jnp.float32)
+        for r in range(tp_count):
+            together = jnp.concatenate([rows_all[r, h] for h in range(heads)], axis=1)
+            acc = acc + jnp.dot(together, weight_cols[r, :, cols], preferred_element_type=jnp.float32)
         finished[:, cols] = acc.astype(finished.dtype)
         for o in range(1, tp_count):
             out_copy(o, c, tp, lax.rem(tp + o, tp_count)).start()
@@ -307,19 +349,33 @@
     for o in range(1, tp_count):
         for c in range(chunks):
             out_copy(o, c, lax.rem(tp - o + tp_count, tp_count), tp).wait_recv()
+    for p in range(2, dc_count, 2):
+        @pl.when(pair < p)
+        def _():
+            for z in range(2):
+                kv_copy(p, z, me).wait_send()
+
+    @pl.when(core == 0)
+    def _():
+        for z in range(2):
+            pair_copy(z, me, me + 1).wait_send()
+
+    for source in range(dc_count - 2):
+        @pl.when(source < pair)
+        def _():
+            hand_copy(core, source, other).wait_send()
+
     for o in range(1, dc_count):
-        @pl.when(me + o < dc_count)
-        def _():
-            for copy in kv_copies(o, me, me + o):
-                copy.wait_send()
-        route_copy(o, me, lax.rem(me + o, dc_count)).wait_send()
+        for h in range(heads):
+            route_copy(o, h, me, lax.rem(me + o, dc_count)).wait_send()
     for o in range(1, tp_count):
         peer = lax.rem(tp + o, tp_count)
         weight_copy(o, tp, peer).wait_send()
-        share_copy(o, tp, peer).wait_send()
+        for h in range(heads):
+            share_copy(o, h, tp, peer).wait_send()
         for p in range(1, SHARERS):
-            pass_copy(o, p, lax.rem(tp - o + tp_count, tp_count), my_part,
-                      base + lax.rem(lane + p, SHARERS)).wait_send()
+            pass_copy(o, p, lax.rem(tp - o + tp_count, tp_count), part_of(sharing(o)[0]),
+                      sharer(o, p)).wait_send()
         for c in range(chunks):
             out_copy(o, c, tp, peer).wait_send()
 
@@ -327,35 +383,39 @@
 def in_one_kernel(dc_count, tp_count, queries, keys, values, lengths, mlp_owner, out_weight, residual):
     rows, columns = queries.shape
     depth, width = out_weight.shape
+    heads = columns // HEAD_SIZE
     capacity = (rows + dc_count - 1) // dc_count + rows // dc_count
     chunks = width // tp_count // COLUMN_CHUNK
     half = jnp.bfloat16
     dma = pltpu.SemaphoreType.DMA
     vmem, smem = pl.BlockSpec(memory_space=pltpu.VMEM), pl.BlockSpec(memory_space=pltpu.SMEM)
+    anywhere = pl.BlockSpec(memory_space=pl.ANY)
     summed = pl.pallas_call(
         functools.partial(fused, dc_count, tp_count),
         out_shape=jax.ShapeDtypeStruct((rows // tp_count, width), half),
-        in_specs=[smem, vmem, vmem, vmem, vmem, pl.BlockSpec(memory_space=pl.ANY)],
+        in_specs=[smem, vmem, anywhere, anywhere, anywhere, anywhere],
         out_specs=vmem,
         scratch_shapes=[
-            pltpu.VMEM((dc_count * rows, HEAD_SIZE), half),
-            pltpu.VMEM((dc_count * rows, HEAD_SIZE), half),
             pltpu.VMEM((rows, columns), half),
-            pltpu.VMEM((dc_count * capacity, columns), half),
-            pltpu.VMEM((dc_count * capacity, columns), half),
-            pltpu.VMEM((tp_count, rows, columns), half),
+            pltpu.VMEM((2, dc_count * rows, HEAD_SIZE), half),
+            pltpu.VMEM((heads, rows, HEAD_SIZE), half),
+            pltpu.VMEM((heads, dc_count * capacity, HEAD_SIZE), half),
+            pltpu.VMEM((heads, dc_count * capacity, HEAD_SIZE), half),
+            pltpu.VMEM((tp_count, heads, rows, HEAD_SIZE), half),
             pltpu.VMEM((tp_count, depth, width // tp_count), half),
             pltpu.VMEM((rows, width // tp_count), half),
-            dma((dc_count, 2)), dma((dc_count, 2)),
+            dma((dc_count // 2, 2)), dma((dc_count,)),
             dma((dc_count,)), dma((dc_count,)),
-            dma((tp_count,)), dma((tp_count,)),
+            dma((2,)), dma((2,)),
+            dma((dc_count, heads)), dma((dc_count, heads)),
+            dma((tp_count, heads)), dma((tp_count, heads)),
             dma((tp_count,)), dma((tp_count,)),
             dma((tp_count, SHARERS)), dma((tp_count, SHARERS)),
-            dma(()),
+            dma(()), dma((3,)),
             dma((tp_count, chunks)), dma((tp_count, chunks)),
         ],
         compiler_params=pltpu.CompilerParams(
-            collective_id=0, has_side_effects=True, vmem_limit_bytes=40 * 2**20),
+            collective_id=0, has_side_effects=True, vmem_limit_bytes=60 * 2**20),
     )(lengths, mlp_owner.reshape(dc_count, rows), queries, keys, values, out_weight)
     return (summed.astype(jnp.float32) + residual.astype(jnp.float32)).astype(half)
 

time: 55.1 us -> 44.5 us (0.81)
  Pallas kernels: 48.3 us -> 41 us
  local copies, waits for them, and re-layouts: 5.69 us -> 1.42 us
  other arithmetic: 0.84 us -> 1.83 us
    pallas_call x1, Pallas kernels: 48.3 us -> 41 us  [in_one_kernel(): pl.pallas_call(functools.partial(fused, dc_count, tp_count), out_shape=ja...]
    unnamed x12 -> x2, local copies, waits for them, and re-layouts: 4.93 us -> 0.01 us
    convert_element_type x1, other arithmetic: 0.84 us -> 1.83 us  [in_one_kernel(): (summed.astype(jnp.float32) + residual.astype(jnp.float32)).astype(half)]
    reshape x1, local copies, waits for them, and re-layouts: 0.77 us -> 1.42 us  [in_one_kernel(): mlp_owner.reshape(dc_count, rows)]
where the time goes in v2:
time: 44.5 us; the launch traced here: 44.2 us
  Pallas kernels  41 us (92%)
  other arithmetic  1.83 us (4%)
  local copies, waits for them, and re-layouts  1.42 us (3%)
    pallas_call x1, Pallas kernels, in_one_kernel(): pl.pallas_call(functools.partial(fused, dc_count, tp_count), out_shape=ja...  41 us
    convert_element_type x1, other arithmetic, in_one_kernel(): (summed.astype(jnp.float32) + residual.astype(jnp.float32)).astype(half)  1.83 us
    reshape x1, local copies, waits for them, and re-layouts, in_one_kernel(): mlp_owner.reshape(dc_count, rows)  1.42 us

profile of v2, /device:TPU:0, one launch (start us, length us, event | category | flops | bytes accessed | tf_op | source)
XLA Modules:
  0.0 44.2 jit_solution(16391032548373420960)
XLA Ops:
  0.0 0.0 copy-start
  0.0 1.4 %reshape.3.owners = s32[8,192]{1,0:T(8,128)} reshape(s32[1536]{0:T(1024)} %param.11) | data formatting | bytes 12288 | tf_op jit(solution)/shard_map/reshape | solution.py:419
  1.4 41.0 %shard_map.73 = bf16[48,4096]{1,0:T(8,128)(2,1)} custom-call(s32[24]{0:T(128)} %lengths.1, s32[8,192]{1,0:T(8,128)} %reshape.3.owners, bf16[192,256]{1,0:T(8,128)(2,1)} %queries.1, bf16[192,256]{1,0:T(8,128)(2,1)} %keys.1, bf16[192,256]{1,0:T(8,128)(2,1)} %values.1, bf16[256,4096]{1,0:T(8,128)(2,1)} %weight.1), custom_call_target="tpu_custom_call" | custom-call | tf_op jit(solution)/shard_map/pallas_call | solution.py:393
  42.4 0.0 copy-done
  42.4 1.8 %add_convert_fusion = bf16[48,4096]{1,0:T(8,128)(2,1)} fusion(bf16[48,4096]{1,0:T(8,128)(2,1)S(1)} %copy-done, bf16[48,4096]{1,0:T(8,128)(2,1)} %shard_map.73), kind=kLoop, calls=%fused_computation | loop fusion | flops 786432 | bytes 1179648 | tf_op jit(solution)/shard_map/convert_element_type | solution.py:420
Async XLA Ops:
  0.0 42.4 %copy-start = (bf16[48,4096]{1,0:T(8,128)(2,1)S(1)}, bf16[48,4096]{1,0:T(8,128)(2,1)}, u32[]{:S(2)}) copy-start(bf16[48,4096]{1,0:T(8,128)(2,1)} %param.13) | copy-start | bytes 1179652
